TPU v7x, 32 devices: a whole 2x2x4 slice. The times are simulated.
32 devices in a mesh: expert: 8 (over z, y), replica: 4 (over x, core).
Axes of the slice: x: 2, y: 2, z: 4, core: 2. Of those that a mesh axis runs over, the one named last changes fastest.
Arguments:
- inputs: bfloat16 [2, 2048, 2048], P(None, ('expert', 'replica')), may hold values from -6 to 6
- out_grads: bfloat16 [2, 2048, 2048], P(None, ('expert', 'replica')), may hold values from -6 to 6
- routes: int32 [2, 2048, 1], P(None, ('expert', 'replica')), may hold values from 0 to 7; in each aligned block of 64 rows (0 to 63, 64 to 127, ..., all dimensions but the last counted through in order) at most 16 rows name the same one
- gate_probs: float32 [2, 2048, 1], P(None, ('expert', 'replica')), may hold values from 0.2 to 1
- master: float32 [8, 256, 6144], P('expert', 'replica'), may hold values from -6 to 6
- moment: float32 [8, 256, 6144], P('expert', 'replica'), may hold values from -3 to 3
- second: bfloat16 [8, 256, 6144], P('expert', 'replica'), may hold values from 0.0099487305 to 1
Outputs:
- in_grads: bfloat16 [2, 2048, 2048], P(None, ('expert', 'replica'))
- new_master: float32 [8, 256, 6144], P('expert', 'replica')
- new_moment: float32 [8, 256, 6144], P('expert', 'replica')
- new_second: bfloat16 [8, 256, 6144], P('expert', 'replica')
Inputs may be any that keep to these rules, and one draw needn't show every extreme that they name: `routes`: each token names exactly one expert. In each micro-batch no expert is named by more than 16 tokens of one block of 64 tokens, a bound that some block reaches.
All inputs are finite; a program needn't handle non-finite values.
Results may differ from a plain program's by a relative error of at most 0.028.
Values may be sent and summed in bfloat16 or wider, within the bound.
A program may use at most 64 MiB of HBM per device.

v0:
```python
import math

import jax
import jax.numpy as jnp
from jax import lax
from jax.sharding import PartitionSpec as P

beta_one = 0.9
beta_two = 0.95
learning_rate = 0.01
decay_rate = 0.1
epsilon = 1e-08


def slot_positions(route_pairs, capacity):
    pair_count = route_pairs.shape[-1]
    positions = jnp.arange(pair_count, dtype=jnp.int32)
    same_route = (route_pairs[..., :, None] == route_pairs[..., None, :]) & (
        positions[None, :] < positions[:, None]
    )
    earlier = jnp.sum(same_route.astype(jnp.int32), axis=-1)
    return route_pairs * capacity + earlier


def expert_rows(rows_in, rows_grad, weights):
    model_width = rows_in.shape[-1]
    scale_in = 1.0 / math.sqrt(model_width)
    scale_hidden = 1.0 / math.sqrt(weights.shape[0])
    w_gate = weights[:, :model_width]
    w_up = weights[:, model_width : 2 * model_width]
    w_down = weights[:, 2 * model_width :]
    gate_value = jnp.dot(rows_in, w_gate.T, preferred_element_type=jnp.float32) * scale_in
    up_value = jnp.dot(rows_in, w_up.T, preferred_element_type=jnp.float32) * scale_in
    sigmoid_gate = jax.nn.sigmoid(gate_value)
    activated = gate_value * sigmoid_gate
    hidden = (activated * up_value).astype(jnp.bfloat16)
    hidden_grad = jnp.dot(rows_grad, w_down.T, preferred_element_type=jnp.float32) * scale_hidden
    up_grad = (hidden_grad * activated).astype(jnp.bfloat16)
    gate_grad = (
        hidden_grad * up_value * sigmoid_gate * (1.0 + gate_value * (1.0 - sigmoid_gate))
    ).astype(jnp.bfloat16)
    slot_grads = (
        jnp.dot(gate_grad, w_gate, preferred_element_type=jnp.float32)
        + jnp.dot(up_grad, w_up, preferred_element_type=jnp.float32)
    ) * scale_in
    return (hidden, gate_grad, up_grad, slot_grads.astype(jnp.bfloat16))


def gate_up_terms(rows_in, gate_grad, up_grad):
    scale_in = 1.0 / math.sqrt(rows_in.shape[-1])
    gate_term = jnp.dot(gate_grad.T, rows_in, preferred_element_type=jnp.float32) * scale_in
    up_term = jnp.dot(up_grad.T, rows_in, preferred_element_type=jnp.float32) * scale_in
    return jnp.concatenate([gate_term, up_term], axis=1)


def down_terms(rows_grad, hidden):
    scale_hidden = 1.0 / math.sqrt(hidden.shape[-1])
    return jnp.dot(hidden.T, rows_grad, preferred_element_type=jnp.float32) * scale_hidden


def adamw_step(master, moment, second, grad_sum):
    new_moment = beta_one * moment + (1.0 - beta_one) * grad_sum
    second_sum = beta_two * second.astype(jnp.float32) + (1.0 - beta_two) * grad_sum * grad_sum
    new_master = master - learning_rate * (
        new_moment / (jnp.sqrt(second_sum) + epsilon) + decay_rate * master
    )
    return (new_master, new_moment, second_sum.astype(jnp.bfloat16))


def on_device(inputs, out_grads, routes, gate_probs, master, moment, second):
    experts = lax.axis_size("expert")
    batches, tokens, model_width = inputs.shape
    top_count = routes.shape[2]
    pair_count = tokens * top_count
    capacity = max(2, 2 * pair_count // experts)
    weights = lax.all_gather(master[0].astype(jnp.bfloat16), "replica", axis=0, tiled=True)
    route_pairs = routes.reshape(batches, pair_count)
    slot_ids = slot_positions(route_pairs, capacity)
    slot_range = jnp.arange(experts * capacity, dtype=jnp.int32)
    onehot = (slot_ids[:, None, :] == slot_range[None, :, None]).astype(jnp.bfloat16)
    onehot = onehot.reshape(batches, experts, capacity, pair_count)
    pair_inputs = jnp.repeat(inputs, top_count, axis=1)
    pair_grads = (
        gate_probs.reshape(batches, pair_count)[..., None]
        * jnp.repeat(out_grads, top_count, axis=1).astype(jnp.float32)
    ).astype(jnp.bfloat16)
    send_in = jnp.einsum(
        "besp,bpd->ebsd", onehot, pair_inputs, preferred_element_type=jnp.float32
    ).astype(jnp.bfloat16)
    send_grad = jnp.einsum(
        "besp,bpd->ebsd", onehot, pair_grads, preferred_element_type=jnp.float32
    ).astype(jnp.bfloat16)
    arrived_in, arrived_grad = (
        lax.all_to_all(send_in, "expert", split_axis=0, concat_axis=0, tiled=True),
        lax.all_to_all(send_grad, "expert", split_axis=0, concat_axis=0, tiled=True),
    )
    all_in = arrived_in.reshape(experts * batches * capacity, model_width)
    all_grad = arrived_grad.reshape(experts * batches * capacity, model_width)
    all_hidden, all_gate, all_up, slot_grads = expert_rows(all_in, all_grad, weights)
    returned_rows = lax.all_to_all(
        slot_grads.reshape(experts, batches, capacity, model_width),
        "expert",
        split_axis=0,
        concat_axis=0,
        tiled=True,
    )
    pair_back = jnp.einsum(
        "besp,ebsd->bpd", onehot, returned_rows, preferred_element_type=jnp.float32
    )
    in_grads = jnp.sum(pair_back.reshape(batches, tokens, top_count, model_width), axis=2).astype(
        jnp.bfloat16
    )
    grad_sum = lax.psum_scatter(
        jnp.concatenate(
            [gate_up_terms(all_in, all_gate, all_up), down_terms(all_grad, all_hidden)], axis=1
        ).astype(jnp.bfloat16),
        "replica",
        scatter_dimension=0,
        tiled=True,
    ).astype(jnp.float32)
    new_master, new_moment, new_second = adamw_step(master[0], moment[0], second[0], grad_sum)
    return (in_grads, new_master[None], new_moment[None], new_second[None])


def solution(mesh):
    placed = (
        P(None, ("expert", "replica"), None),
        P(None, ("expert", "replica"), None),
        P(None, ("expert", "replica"), None),
        P(None, ("expert", "replica"), None),
        P("expert", "replica", None),
        P("expert", "replica", None),
        P("expert", "replica", None),
    )
    return jax.shard_map(
        on_device,
        mesh=mesh,
        in_specs=placed,
        out_specs=(
            P(None, ("expert", "replica"), None),
            P("expert", "replica", None),
            P("expert", "replica", None),
            P("expert", "replica", None),
        ),
        check_vma=False,
    )
```

profile of v0, /device:TPU:0, one launch (start us, length us, event | category | flops | bytes accessed | tf_op | source)
XLA Modules:
  0.0 127.8 jit_solution(13689522808702070237)
XLA Ops:
  7.2 0.0 copy-start
  7.2 0.0 copy-start.3
  7.2 0.0 all-gather.2.cloned.1.call-start
  7.2 2.4 %bitcast_convert_fusion = bf16[64,6144]{1,0:T(8,128)(2,1)} fusion(f32[1,64,6144]{2,1,0:T(8,128)} %param.11), kind=kLoop, calls=%fused_computation.22 | loop fusion | flops 393216 | bytes 2359296 | tf_op jit(solution)/shard_map/convert_element_type | solution.py:76
  9.6 0.0 all-gather.2.cloned.1.call-update
  9.7 0.0 copy-done.3
  9.7 0.2 convert_reduce_fusion
  9.9 0.0 copy-done
  9.9 0.5 fusion.6
  10.4 0.0 copy-start.4
  10.4 0.0 copy-start.5
  10.4 1.0 copy.19
  11.5 7.3 %all-to-all-start.1 = ((bf16[8,2,16,2048]{3,2,1,0:T(8,128)(2,1)}), bf16[8,2,16,2048]{3,2,1,0:T(8,128)(2,1)S(1)}, u32[]{:S(2)}, u32[]{:S(2)}) async-start(bf16[8,2,16,2048]{3,2,1,0:T(8,128)(2,1)} %copy.19), calls=%async_computation.1 | async-start | bytes 2097152 | tf_op jit(solution)/shard_map/all_to_all | solution.py:94
  18.7 0.0 copy-done.4
  18.7 0.0 copy-done.5
  18.8 0.5 fusion.5
  19.3 1.0 copy.18
  20.3 24.2 %all-to-all-done.1 = bf16[8,2,16,2048]{3,2,1,0:T(8,128)(2,1)S(1)} async-done(((bf16[8,2,16,2048]{3,2,1,0:T(8,128)(2,1)}), bf16[8,2,16,2048]{3,2,1,0:T(8,128)(2,1)S(1)}, u32[]{:S(2)}, u32[]{:S(2)}) %all-to-all-start.1) | async-done | bytes 1048608 | tf_op jit(solution)/shard_map/all_to_all | solution.py:94
  44.5 3.6 %all-to-all-start = ((bf16[8,2,16,2048]{3,2,1,0:T(8,128)(2,1)}), bf16[8,2,16,2048]{3,2,1,0:T(8,128)(2,1)S(1)}, u32[]{:S(2)}, u32[]{:S(2)}) async-start(bf16[8,2,16,2048]{3,2,1,0:T(8,128)(2,1)} %copy.18), calls=%async_computation | async-start | bytes 2097152 | tf_op jit(solution)/shard_map/all_to_all | solution.py:95
  48.1 0.0 reduce-scatter.2.cloned.1.call-start
  48.1 0.0 all-gather.2.cloned.1.call-done
  48.2 1.7 %convolution_multiply_fusion.3 = f32[256,256]{1,0:T(8,128)S(1)} fusion(bf16[256,2048]{1,0:T(8,128)(2,1)S(1)} %bitcast.66, bf16[256,6144]{1,0:T(8,128)(2,1)} %all-gather.2.cloned.1.call-done), kind=kOutput, calls=%fused_computation.27 | convolution fusion | flops 268500992 | bytes 2359296 | tf_op jit(solution)/shard_map/dot_general | solution.py:32
  49.9 1.7 %convolution_multiply_fusion.4 = f32[256,256]{1,0:T(8,128)S(1)} fusion(bf16[256,2048]{1,0:T(8,128)(2,1)S(1)} %bitcast.67, bf16[256,6144]{1,0:T(8,128)(2,1)} %all-gather.2.cloned.1.call-done), kind=kOutput, calls=%fused_computation.28 | convolution fusion | flops 268500992 | bytes 2359296 | tf_op jit(solution)/shard_map/dot_general | solution.py:33
  51.6 22.5 %all-to-all-done = bf16[8,2,16,2048]{3,2,1,0:T(8,128)(2,1)S(1)} async-done(((bf16[8,2,16,2048]{3,2,1,0:T(8,128)(2,1)}), bf16[8,2,16,2048]{3,2,1,0:T(8,128)(2,1)S(1)}, u32[]{:S(2)}, u32[]{:S(2)}) %all-to-all-start) | async-done | bytes 1048608 | tf_op jit(solution)/shard_map/all_to_all | solution.py:95
  74.1 0.5 fusion.4
  74.6 1.7 %multiply_convert_fusion.2 = (bf16[256,256]{1,0:T(8,128)(2,1)S(1)}, bf16[256,256]{1,0:T(8,128)(2,1)S(1)}) fusion(f32[256,256]{1,0:T(8,128)S(1)} %convolution_multiply_fusion.3, f32[256,256]{1,0:T(8,128)S(1)} %convolution_multiply_fusion.4, bf16[256,2048]{1,0:T(8,128)(2,1)S(1)} %bitcast.72, bf16[256,6144]{1,0:T(8,128)(2,1)} %all-gather.2.cloned.1.call-done), kind=kOutput, calls=%fused_computation.44 | convolution fusion | flops 269352960 | bytes 2883584 | tf_op jit(solution)/shard_map/dot_general | solution.py:37
  76.3 0.5 fusion.3
  76.8 0.5 fusion.2
  77.2 1.8 %pad_maximum_fusion = bf16[256,6144]{1,0:T(8,128)(2,1)} fusion(bf16[256,2048]{1,0:T(8,128)(2,1)S(1)} %fusion.4, bf16[256,2048]{1,0:T(8,128)(2,1)S(1)} %fusion.3, bf16[256,2048]{1,0:T(8,128)(2,1)S(1)} %fusion.2), kind=kLoop, calls=%fused_computation | loop fusion | flops 9437184 | bytes 6291456 | tf_op jit(solution)/shard_map/concatenate | solution.py:114
  79.0 0.0 reduce-scatter.2.cloned.1.call-update
  79.0 1.7 %fusion.16 = f32[256,2048]{1,0:T(8,128)S(1)} fusion(bf16[256,256]{1,0:T(8,128)(2,1)S(1)} %get-tuple-element.8, bf16[256,6144]{1,0:T(8,128)(2,1)} %all-gather.2.cloned.1.call-done), kind=kOutput, calls=%fused_computation.33 | convolution fusion | flops 268435456 | bytes 3276800 | tf_op jit(solution)/shard_map/dot_general | solution.py:43
  80.7 1.7 %fusion.1 = bf16[256,2048]{1,0:T(8,128)(2,1)S(1)} fusion(f32[256,2048]{1,0:T(8,128)S(1)} %fusion.16, bf16[256,256]{1,0:T(8,128)(2,1)S(1)} %get-tuple-element.7, bf16[256,6144]{1,0:T(8,128)(2,1)} %all-gather.2.cloned.1.call-done), kind=kOutput, calls=%fused_computation.6 | convolution fusion | flops 270008320 | bytes 4325376 | tf_op jit(solution)/shard_map/dot_general | solution.py:44
  82.4 0.0 copy-start.1
  82.4 0.0 copy-start.2
  82.5 29.5 %all_to_all.15 = bf16[8,2,16,2048]{3,2,1,0:T(8,128)(2,1)S(1)} all-to-all(bf16[8,2,16,2048]{3,2,1,0:T(8,128)(2,1)S(1)} %bitcast.70), channel_id=1, replica_groups=mesh['expert'=8,'replica'=4] {'expert'}, dimensions={0} | all-to-all | bytes 2097152 | tf_op jit(solution)/shard_map/all_to_all | solution.py:100
  111.9 1.2 fusion.7
  113.1 3.0 %reduce-scatter.2.cloned.1.call-done = bf16[64,6144]{1,0:T(8,128)(2,1)} async-done(((bf16[256,6144]{1,0:T(8,128)(2,1)}), bf16[64,6144]{1,0:T(8,128)(2,1)}) %reduce-scatter.2.cloned.1.call-update) | async-done | bytes 786448 | tf_op jit(solution)/shard_map/reduce_scatter | solution.py:113
  116.2 0.0 copy-done.1
  116.2 0.0 copy-done.2
  116.2 4.8 %fusion.21 = (f32[1,64,6144]{2,1,0:T(8,128)}, f32[1,64,6144]{2,1,0:T(8,128)}, bf16[1,64,6144]{2,1,0:T(8,128)(2,1)}) fusion(bf16[64,6144]{1,0:T(8,128)(2,1)} %reduce-scatter.2.cloned.1.call-done, f32[1,64,6144]{2,1,0:T(8,128)} %param.12, bf16[1,64,6144]{2,1,0:T(8,128)(2,1)S(1)} %copy-done.2, f32[1,64,6144]{2,1,0:T(8,128)S(1)} %copy-done.1), kind=kLoop, calls=%fused_computation.38 | loop fusion | flops 6291456 | bytes 8650752 | tf_op jit(solution)/shard_map/broadcast_in_dim | solution.py:122
  (3 shorter events, 0.0 us)
Async XLA Ops:
  7.2 2.7 %copy-start = (bf16[2,64,2048]{2,1,0:T(8,128)(2,1)S(1)}, bf16[2,64,2048]{2,1,0:T(8,128)(2,1)}, u32[]{:S(2)}) copy-start(bf16[2,64,2048]{2,1,0:T(8,128)(2,1)} %param.7) | copy-start | bytes 1572868
  7.2 2.5 %copy-start.3 = (s32[2,64,1]{1,2,0:T(1,128)S(1)}, s32[2,64,1]{1,2,0:T(1,128)}, u32[]{:S(2)}) copy-start(s32[2,64,1]{1,2,0:T(1,128)} %param.9) | copy-start | bytes 1540
  7.2 41.0 %all-gather.2.cloned.1.call-start = ((), (), s32[]{:S(2)}) async-start(), calls=%async_computation.4 | async-start | bytes 3932160 | tf_op jit(solution)/shard_map/all_gather | solution.py:76
  10.4 8.3 %copy-start.4 = (bf16[2,64,2048]{2,1,0:T(8,128)(2,1)S(1)}, bf16[2,64,2048]{2,1,0:T(8,128)(2,1)}, u32[]{:S(2)}) copy-start(bf16[2,64,2048]{2,1,0:T(8,128)(2,1)} %param.8) | copy-start | bytes 1572868
  10.4 8.3 %copy-start.5 = (f32[2,64,1]{1,2,0:T(1,128)S(1)}, f32[2,64,1]{1,2,0:T(1,128)}, u32[]{:S(2)}) copy-start(f32[2,64,1]{1,2,0:T(1,128)} %param.10) | copy-start | bytes 1540
  11.5 33.0 %all-to-all-start.1 = ((bf16[8,2,16,2048]{3,2,1,0:T(8,128)(2,1)}), bf16[8,2,16,2048]{3,2,1,0:T(8,128)(2,1)S(1)}, u32[]{:S(2)}, u32[]{:S(2)}) async-start(bf16[8,2,16,2048]{3,2,1,0:T(8,128)(2,1)} %copy.19), calls=%async_computation.1 | async-start | bytes 2097152 | tf_op jit(solution)/shard_map/all_to_all | solution.py:94
  44.5 29.5 %all-to-all-start = ((bf16[8,2,16,2048]{3,2,1,0:T(8,128)(2,1)}), bf16[8,2,16,2048]{3,2,1,0:T(8,128)(2,1)S(1)}, u32[]{:S(2)}, u32[]{:S(2)}) async-start(bf16[8,2,16,2048]{3,2,1,0:T(8,128)(2,1)} %copy.18), calls=%async_computation | async-start | bytes 2097152 | tf_op jit(solution)/shard_map/all_to_all | solution.py:95
  48.1 68.1 %reduce-scatter.2.cloned.1.call-start = ((), (), s32[]{:S(2)}) async-start(), calls=%async_computation.5 | async-start | bytes 3932160 | tf_op jit(solution)/shard_map/reduce_scatter | solution.py:113
  82.4 33.8 %copy-start.1 = (f32[1,64,6144]{2,1,0:T(8,128)S(1)}, f32[1,64,6144]{2,1,0:T(8,128)}, u32[]{:S(2)}) copy-start(f32[1,64,6144]{2,1,0:T(8,128)} %param.11) | copy-start | bytes 4718596
  82.4 33.7 %copy-start.2 = (bf16[1,64,6144]{2,1,0:T(8,128)(2,1)S(1)}, bf16[1,64,6144]{2,1,0:T(8,128)(2,1)}, u32[]{:S(2)}) copy-start(bf16[1,64,6144]{2,1,0:T(8,128)(2,1)} %param.13) | copy-start | bytes 2359300
Sparse Core Ops, SparseCore 0:
  10.2 31.2 all-gather.1
  79.2 36.9 reduce-scatter.1
where the time goes:
time: 128 us
  waiting for transfers between devices  49.8 us (39%)
  blocking collectives  29.5 us (23%)
  between operations  14.2 us (11%)
  matrix products  12.1 us (9%)
  starting transfers between devices  10.9 us (9%)
  other arithmetic  9.19 us (7%)
  local copies, waits for them, and re-layouts  2.12 us (2%)
    all_to_all x1, blocking collectives, on_device(): lax.all_to_all(slot_grads.reshape(experts, batches, capacity, model_width...  29.5 us
    all_to_all x1, waiting for transfers between devices, on_device(): lax.all_to_all(send_in, 'expert', split_axis=0, concat_axis=0, tiled=True)  24.2 us
    all_to_all x1, waiting for transfers between devices, on_device(): lax.all_to_all(send_grad, 'expert', split_axis=0, concat_axis=0, tiled=True)  22.5 us
    all_to_all x1, starting transfers between devices, on_device(): lax.all_to_all(send_in, 'expert', split_axis=0, concat_axis=0, tiled=True)  7.28 us
    broadcast_in_dim x1, other arithmetic, on_device(): return (in_grads, new_master[None], new_moment[None], new_second[None])  4.77 us
    all_to_all x1, starting transfers between devices, on_device(): lax.all_to_all(send_grad, 'expert', split_axis=0, concat_axis=0, tiled=True)  3.59 us
    reduce_scatter x1, waiting for transfers between devices, on_device(): lax.psum_scatter(jnp.concatenate([gate_up_terms(all_in, all_gate, all_up)...  3.05 us
  transfers between devices with their start and end apart: 4, of which 3 were waited for; matrix products, arithmetic and copies ran while one was open for 9% of the time, Pallas kernels for 0%

commit v1 on v0

--- a/solution.py
+++ b/solution.py
@@ -1,8 +1,11 @@
+import functools
 import math
 
 import jax
 import jax.numpy as jnp
 from jax import lax
+from jax.experimental import pallas as pl
+from jax.experimental.pallas import tpu as pltpu
 from jax.sharding import PartitionSpec as P
 
 beta_one = 0.9
@@ -10,6 +13,8 @@
 learning_rate = 0.01
 decay_rate = 0.1
 epsilon = 1e-08
+MESH = pl.DeviceIdType.MESH
+NT = (((1,), (1,)), ((), ()))
 
 
 def slot_positions(route_pairs, capacity):
@@ -67,7 +72,7 @@
     return (new_master, new_moment, second_sum.astype(jnp.bfloat16))
 
 
-def on_device(inputs, out_grads, routes, gate_probs, master, moment, second):
+def on_device_plain(inputs, out_grads, routes, gate_probs, master, moment, second):
     experts = lax.axis_size("expert")
     batches, tokens, model_width = inputs.shape
     top_count = routes.shape[2]
@@ -122,6 +127,300 @@
     return (in_grads, new_master[None], new_moment[None], new_second[None])
 
 
+def layer_kernel(
+    experts,
+    capacity,
+    in_ref,
+    og_ref,
+    routes_ref,
+    probs_ref,
+    master_ref,
+    ingrad_ref,
+    grad_ref,
+    send,
+    recv,
+    weights,
+    slots,
+    ret,
+    pick_back,
+    terms,
+    part,
+    sib,
+    chip_sum,
+    from_x,
+    dsend,
+    drecv,
+    bsend,
+    brecv,
+    wsend,
+    wrecv,
+    rsend,
+    rrecv,
+):
+    batches, tokens, width = in_ref.shape
+    units = weights.shape[2]
+    total_units = 4 * units
+    rows = experts * capacity
+    scale_in = 1.0 / math.sqrt(width)
+    scale_hidden = 1.0 / math.sqrt(total_units)
+    e = lax.axis_index("expert")
+    r = lax.axis_index("replica")
+    chip_x, core = r // 2, lax.rem(r, 2)
+    r_sib = chip_x * 2 + (1 - core)
+    r_x = (1 - chip_x) * 2 + core
+    r_far = (1 - chip_x) * 2 + (1 - core)
+
+    barrier = pltpu.get_barrier_semaphore()
+
+    def greet(k, c):
+        pl.semaphore_signal(
+            barrier, inc=1, device_id=(lax.rem(e + k, experts), r), device_id_type=MESH
+        )
+        return c
+
+    lax.fori_loop(1, experts, greet, 0)
+    for other in (r_sib, r_x):
+        pl.semaphore_signal(barrier, inc=1, device_id=(e, other), device_id_type=MESH)
+
+    def dispatch(which, b, k):
+        peer = lax.rem(e + k, experts)
+        return pltpu.make_async_remote_copy(
+            src_ref=send.at[which, b, peer],
+            dst_ref=recv.at[which, b, e],
+            send_sem=dsend.at[which, b, k - 1],
+            recv_sem=drecv.at[which, b, k - 1],
+            device_id=(peer, r),
+            device_id_type=MESH,
+        )
+
+    def give_back(b, k):
+        peer = lax.rem(e + k, experts)
+        return pltpu.make_async_remote_copy(
+            src_ref=slots.at[b, peer],
+            dst_ref=ret.at[b, e],
+            send_sem=bsend.at[b, k - 1],
+            recv_sem=brecv.at[b, k - 1],
+            device_id=(peer, r),
+            device_id_type=MESH,
+        )
+
+    def weight_copy(kind, k):
+        block = (r, r, r_x)[kind]
+        target = (r_sib, r_x, r_sib)[kind]
+        return pltpu.make_async_remote_copy(
+            src_ref=weights.at[k, block],
+            dst_ref=weights.at[k, block],
+            send_sem=wsend.at[kind, k],
+            recv_sem=wrecv.at[kind, k],
+            device_id=(e, target),
+            device_id_type=MESH,
+        )
+
+    def grad_copy(kind, k):
+        if kind == 2:
+            source, target, place = chip_sum.at[k], r_x, from_x.at[k]
+        else:
+            source, target = part.at[k, (r_far, r_sib)[kind]], r_sib
+            place = sib.at[kind, k]
+        return pltpu.make_async_remote_copy(
+            src_ref=source,
+            dst_ref=place,
+            send_sem=rsend.at[kind, k],
+            recv_sem=rrecv.at[kind, k],
+            device_id=(e, target),
+            device_id_type=MESH,
+        )
+
+    def each_peer(step):
+        def body(k, c):
+            step(k)
+            return c
+
+        lax.fori_loop(1, experts, body, 0)
+
+    first = lax.broadcasted_iota(jnp.int32, (tokens, tokens), 0)
+    second = lax.broadcasted_iota(jnp.int32, (tokens, tokens), 1)
+
+    def pick(b):
+        route_col = routes_ref[b].astype(jnp.float32)
+        route_row = jnp.sum(jnp.where(first == second, route_col, 0.0), axis=0, keepdims=True)
+        same = route_col == route_row
+        before_row = jnp.sum(
+            jnp.where(same & (first < second), 1.0, 0.0), axis=0, keepdims=True
+        )
+        before_col = jnp.sum(
+            jnp.where(same & (second < first), 1.0, 0.0), axis=1, keepdims=True
+        )
+        slot_row = route_row * capacity + before_row
+        slot_col = route_col * capacity + before_col
+        by_slot = lax.broadcasted_iota(jnp.int32, (rows, tokens), 0).astype(jnp.float32)
+        by_token = lax.broadcasted_iota(jnp.int32, (tokens, rows), 1).astype(jnp.float32)
+        one_hot = jnp.where(by_slot == slot_row, 1.0, 0.0).astype(jnp.bfloat16)
+        pick_back[b] = jnp.where(by_token == slot_col, 1.0, 0.0).astype(jnp.bfloat16)
+        return one_hot
+
+    def fill(which, b, one_hot):
+        if which == 0:
+            source = in_ref[b]
+        else:
+            source = (probs_ref[b] * og_ref[b].astype(jnp.float32)).astype(jnp.bfloat16)
+        chosen = jnp.dot(one_hot, source, preferred_element_type=jnp.float32)
+        send[which, b] = chosen.astype(jnp.bfloat16).reshape(experts, capacity, width)
+        recv[which, b, e] = send[which, b, e]
+
+    one_hot = pick(0)
+    fill(0, 0, one_hot)
+    pl.semaphore_wait(barrier, experts + 1)
+    each_peer(lambda k: dispatch(0, 0, k).start())
+    for k in range(3):
+        weights[k, r] = master_ref[:, k * width : (k + 1) * width].astype(jnp.bfloat16)
+        weight_copy(1, k).start()
+        weight_copy(0, k).start()
+    fill(1, 0, one_hot)
+    each_peer(lambda k: dispatch(1, 0, k).start())
+    for b in range(1, batches):
+        one_hot = pick(b)
+        for which in range(2):
+            fill(which, b, one_hot)
+            each_peer(lambda k: dispatch(which, b, k).start())
+
+    for k in range(3):
+        weight_copy(1, k).wait_recv()
+        weight_copy(2, k).start()
+    for k in range(3):
+        weight_copy(0, k).wait_recv()
+        weight_copy(2, k).wait_recv()
+
+    def matrix(k):
+        return weights[k].reshape(total_units, width)
+
+    for b in range(batches):
+        each_peer(lambda k: dispatch(0, b, k).wait_recv())
+        x = recv[0, b].reshape(rows, width)
+        gate = lax.dot_general(x, matrix(0), NT, preferred_element_type=jnp.float32) * scale_in
+        up = lax.dot_general(x, matrix(1), NT, preferred_element_type=jnp.float32) * scale_in
+        sig = jax.nn.sigmoid(gate)
+        act = gate * sig
+        each_peer(lambda k: dispatch(1, b, k).wait_recv())
+        g = recv[1, b].reshape(rows, width)
+        hgrad = (
+            lax.dot_general(g, matrix(2), NT, preferred_element_type=jnp.float32) * scale_hidden
+        )
+        up_grad = hgrad * act
+        gate_grad = hgrad * up * sig * (1.0 + gate * (1.0 - sig))
+        gate_low, up_low = gate_grad.astype(jnp.bfloat16), up_grad.astype(jnp.bfloat16)
+        back = (
+            jnp.dot(gate_low, matrix(0), preferred_element_type=jnp.float32)
+            + jnp.dot(up_low, matrix(1), preferred_element_type=jnp.float32)
+        ) * scale_in
+        slots[b] = back.astype(jnp.bfloat16).reshape(experts, capacity, width)
+        each_peer(lambda k: give_back(b, k).start())
+        ret[b, e] = slots[b, e]
+        span = slice(b * rows, (b + 1) * rows)
+        terms[0, :, span] = gate_grad.T.astype(jnp.bfloat16)
+        terms[1, :, span] = up_grad.T.astype(jnp.bfloat16)
+        terms[2, :, span] = (act * up).T.astype(jnp.bfloat16)
+
+    for k in range(3):
+        source = recv[k // 2].reshape(batches * rows, width)
+        total = jnp.dot(terms[k], source, preferred_element_type=jnp.float32)
+        total = total * (scale_hidden if k == 2 else scale_in)
+        part[k] = total.astype(jnp.bfloat16).reshape(4, units, width)
+        grad_copy(0, k).start()
+        grad_copy(1, k).start()
+    for k in range(3):
+        grad_copy(0, k).wait_recv()
+        chip_sum[k] = (
+            part[k, r_x].astype(jnp.float32) + sib[0, k].astype(jnp.float32)
+        ).astype(jnp.bfloat16)
+        grad_copy(2, k).start()
+
+    for b in range(batches):
+        each_peer(lambda k: give_back(b, k).wait_recv())
+        back = jnp.dot(
+            pick_back[b], ret[b].reshape(rows, width), preferred_element_type=jnp.float32
+        )
+        ingrad_ref[b] = back.astype(jnp.bfloat16)
+    for k in range(3):
+        grad_copy(1, k).wait_recv()
+        grad_copy(2, k).wait_recv()
+        grad_ref[:, k * width : (k + 1) * width] = (
+            part[k, r].astype(jnp.float32)
+            + sib[1, k].astype(jnp.float32)
+            + from_x[k].astype(jnp.float32)
+        )
+    for k in range(3):
+        for kind in range(3):
+            weight_copy(kind, k).wait_send()
+            grad_copy(kind, k).wait_send()
+    for b in range(batches):
+        each_peer(lambda k: dispatch(0, b, k).wait_send())
+        each_peer(lambda k: dispatch(1, b, k).wait_send())
+        each_peer(lambda k: give_back(b, k).wait_send())
+
+
+def fused_layer(experts, capacity, inputs, out_grads, routes, gate_probs, master):
+    batches, tokens, width = inputs.shape
+    units = master.shape[0]
+    rows = experts * capacity
+    peers = experts - 1
+    low = jnp.bfloat16
+    whole = pl.BlockSpec(memory_space=pltpu.VMEM)
+    dma = pltpu.SemaphoreType.DMA
+    return pl.pallas_call(
+        functools.partial(layer_kernel, experts, capacity),
+        out_shape=(
+            jax.ShapeDtypeStruct(inputs.shape, low),
+            jax.ShapeDtypeStruct(master.shape, jnp.float32),
+        ),
+        in_specs=[whole] * 5,
+        out_specs=(whole, whole),
+        scratch_shapes=[
+            pltpu.VMEM((2, batches, experts, capacity, width), low),
+            pltpu.VMEM((2, batches, experts, capacity, width), low),
+            pltpu.VMEM((3, 4, units, width), low),
+            pltpu.VMEM((batches, experts, capacity, width), low),
+            pltpu.VMEM((batches, experts, capacity, width), low),
+            pltpu.VMEM((batches, tokens, rows), low),
+            pltpu.VMEM((3, 4 * units, batches * rows), low),
+            pltpu.VMEM((3, 4, units, width), low),
+            pltpu.VMEM((2, 3, units, width), low),
+            pltpu.VMEM((3, units, width), low),
+            pltpu.VMEM((3, units, width), low),
+            dma((2, batches, peers)),
+            dma((2, batches, peers)),
+            dma((batches, peers)),
+            dma((batches, peers)),
+            dma((3, 3)),
+            dma((3, 3)),
+            dma((3, 3)),
+            dma((3, 3)),
+        ],
+        compiler_params=pltpu.CompilerParams(
+            collective_id=0, has_side_effects=True, vmem_limit_bytes=48 * 1024 * 1024
+        ),
+        cost_estimate=pl.CostEstimate(
+            flops=2 * 8 * batches * rows * 4 * units * width,
+            bytes_accessed=8 * master.size,
+            transcendentals=0,
+        ),
+    )(inputs, out_grads, routes, gate_probs, master)
+
+
+def on_device(inputs, out_grads, routes, gate_probs, master, moment, second):
+    experts = lax.axis_size("expert")
+    tokens = inputs.shape[1]
+    capacity = max(2, 2 * tokens * routes.shape[2] // experts)
+    fits = capacity % 16 == 0 and experts * capacity % 128 == 0
+    if routes.shape[2] != 1 or lax.axis_size("replica") != 4 or not fits:
+        return on_device_plain(inputs, out_grads, routes, gate_probs, master, moment, second)
+    in_grads, grad_sum = fused_layer(
+        experts, capacity, inputs, out_grads, routes, gate_probs, master[0]
+    )
+    new_master, new_moment, new_second = adamw_step(master[0], moment[0], second[0], grad_sum)
+    return (in_grads, new_master[None], new_moment[None], new_second[None])
+
+
 def solution(mesh):
     placed = (
         P(None, ("expert", "replica"), None),

time: 128 us -> 90.3 us (0.71)
  the two profiles are of different devices: /device:TPU:0 before, /device:TPU:29 now
where the time goes in v1:
time: 90.3 us; the launch traced here: 90 us
  Pallas kernels  80.4 us (89%)
  local copies, waits for them, and re-layouts  5.84 us (6%)
  other arithmetic  3.13 us (3%)
    pallas_call x1, Pallas kernels, fused_layer(): pl.pallas_call(functools.partial(layer_kernel, experts, capacity), out_sh...  80.4 us
    unnamed x13, local copies, waits for them, and re-layouts  5.84 us
    broadcast_in_dim x1, other arithmetic, on_device(): return (in_grads, new_master[None], new_moment[None], new_second[None])  3.13 us

profile of v1, /device:TPU:29, one launch (start us, length us, event | category | flops | bytes accessed | tf_op | source)
XLA Modules:
  0.0 90.0 jit_solution(15376079665671430999)
XLA Ops:
  0.6 0.8 copy.11.routes_ref
  1.4 0.8 copy.12.probs_ref
  2.2 0.0 copy-start
  2.2 1.4 %copy-done = f32[1,64,6144]{2,1,0:T(8,128)S(1)} copy-done((f32[1,64,6144]{2,1,0:T(8,128)S(1)}, f32[1,64,6144]{2,1,0:T(8,128)}, u32[]{:S(2)}) %copy-start) | copy-done | bytes 1572888
  3.6 0.0 copy-start.1
  3.6 1.0 %copy-done.1 = bf16[2,64,2048]{2,1,0:T(8,128)(2,1)S(1)} copy-done((bf16[2,64,2048]{2,1,0:T(8,128)(2,1)S(1)}, bf16[2,64,2048]{2,1,0:T(8,128)(2,1)}, u32[]{:S(2)}) %copy-start.1) | copy-done | bytes 524312
  4.7 0.0 copy-start.2
  4.7 1.0 %copy-done.2 = bf16[2,64,2048]{2,1,0:T(8,128)(2,1)S(1)} copy-done((bf16[2,64,2048]{2,1,0:T(8,128)(2,1)S(1)}, bf16[2,64,2048]{2,1,0:T(8,128)(2,1)}, u32[]{:S(2)}) %copy-start.2) | copy-done | bytes 524312
  5.7 0.0 copy-start.3
  5.7 0.0 copy-start.4
  5.7 80.4 %shard_map.102 = (bf16[2,64,2048]{2,1,0:T(8,128)(2,1)S(1)}, f32[64,6144]{1,0:T(8,128)S(1)}) custom-call(bf16[2,64,2048]{2,1,0:T(8,128)(2,1)S(1)} %copy-done.1, bf16[2,64,2048]{2,1,0:T(8,128)(2,1)S(1)} %copy-done.2, s32[2,64,1]{2,1,0:T(8,128)S(1)} %copy.11.routes_ref, f32[2,64,1]{2,1,0:T(8,128)S(1)} %copy.12.probs_ref, f32[64,6144]{1,0:T(8,128)S(1)} %bitcast.22), custom_call_target="tpu_custom_call" | custom-call | flops 2147483648 | bytes 3145728 | tf_op jit(solution)/shard_map/pallas_call | solution.py:370
  86.1 0.0 copy-done.3
  86.1 0.0 copy-done.4
  86.1 3.1 %fusion.3 = (f32[1,64,6144]{2,1,0:T(8,128)}, f32[1,64,6144]{2,1,0:T(8,128)}, bf16[1,64,6144]{2,1,0:T(8,128)(2,1)}) fusion(f32[64,6144]{1,0:T(8,128)S(1)} %get-tuple-element.7, f32[1,64,6144]{2,1,0:T(8,128)S(1)} %copy-done.3, bf16[1,64,6144]{2,1,0:T(8,128)(2,1)S(1)} %copy-done.4, f32[1,64,6144]{2,1,0:T(8,128)S(1)} %copy-done), kind=kLoop, calls=%fused_computation.6 | loop fusion | flops 5898240 | bytes 9437184 | tf_op jit(solution)/shard_map/broadcast_in_dim | solution.py:421
  89.2 0.8 copy.14
Async XLA Ops:
  2.2 1.4 %copy-start = (f32[1,64,6144]{2,1,0:T(8,128)S(1)}, f32[1,64,6144]{2,1,0:T(8,128)}, u32[]{:S(2)}) copy-start(f32[1,64,6144]{2,1,0:T(8,128)} %param.11) | copy-start | bytes 4718596
  3.6 1.0 %copy-start.1 = (bf16[2,64,2048]{2,1,0:T(8,128)(2,1)S(1)}, bf16[2,64,2048]{2,1,0:T(8,128)(2,1)}, u32[]{:S(2)}) copy-start(bf16[2,64,2048]{2,1,0:T(8,128)(2,1)} %in_ref.1) | copy-start | bytes 1572868
  4.7 1.0 %copy-start.2 = (bf16[2,64,2048]{2,1,0:T(8,128)(2,1)S(1)}, bf16[2,64,2048]{2,1,0:T(8,128)(2,1)}, u32[]{:S(2)}) copy-start(bf16[2,64,2048]{2,1,0:T(8,128)(2,1)} %og_ref.1) | copy-start | bytes 1572868
  5.7 80.4 %copy-start.3 = (f32[1,64,6144]{2,1,0:T(8,128)S(1)}, f32[1,64,6144]{2,1,0:T(8,128)}, u32[]{:S(2)}) copy-start(f32[1,64,6144]{2,1,0:T(8,128)} %param.12) | copy-start | bytes 4718596
  5.7 80.4 %copy-start.4 = (bf16[1,64,6144]{2,1,0:T(8,128)(2,1)S(1)}, bf16[1,64,6144]{2,1,0:T(8,128)(2,1)}, u32[]{:S(2)}) copy-start(bf16[1,64,6144]{2,1,0:T(8,128)(2,1)} %param.13) | copy-start | bytes 2359300

commit v2 on v1

--- a/solution.py
+++ b/solution.py
@@ -137,6 +137,9 @@
     master_ref,
     ingrad_ref,
     grad_ref,
+    held_in,
+    held_og,
+    held_master,
     send,
     recv,
     weights,
@@ -156,6 +159,7 @@
     wrecv,
     rsend,
     rrecv,
+    load_sem,
 ):
     batches, tokens, width = in_ref.shape
     units = weights.shape[2]
@@ -170,6 +174,17 @@
     r_x = (1 - chip_x) * 2 + core
     r_far = (1 - chip_x) * 2 + (1 - core)
 
+    loads_in = [
+        pltpu.make_async_copy(in_ref.at[b], held_in.at[b], load_sem.at[0, b])
+        for b in range(batches)
+    ]
+    loads_og = [
+        pltpu.make_async_copy(og_ref.at[b], held_og.at[b], load_sem.at[1, b])
+        for b in range(batches)
+    ]
+    load_master = pltpu.make_async_copy(master_ref, held_master, load_sem.at[2, 0])
+    loads_in[0].start()
+
     barrier = pltpu.get_barrier_semaphore()
 
     def greet(k, c):
@@ -181,6 +196,11 @@
     lax.fori_loop(1, experts, greet, 0)
     for other in (r_sib, r_x):
         pl.semaphore_signal(barrier, inc=1, device_id=(e, other), device_id_type=MESH)
+    load_master.start()
+    loads_og[0].start()
+    for b in range(1, batches):
+        loads_in[b].start()
+        loads_og[b].start()
 
     def dispatch(which, b, k):
         peer = lax.rem(e + k, experts)
@@ -242,8 +262,8 @@
     second = lax.broadcasted_iota(jnp.int32, (tokens, tokens), 1)
 
     def pick(b):
-        route_col = routes_ref[b].astype(jnp.float32)
-        route_row = jnp.sum(jnp.where(first == second, route_col, 0.0), axis=0, keepdims=True)
+        route_row = routes_ref[b].astype(jnp.float32)
+        route_col = jnp.sum(jnp.where(first == second, route_row, 0.0), axis=1, keepdims=True)
         same = route_col == route_row
         before_row = jnp.sum(
             jnp.where(same & (first < second), 1.0, 0.0), axis=0, keepdims=True
@@ -261,9 +281,12 @@
 
     def fill(which, b, one_hot):
         if which == 0:
-            source = in_ref[b]
+            loads_in[b].wait()
+            source = held_in[b]
         else:
-            source = (probs_ref[b] * og_ref[b].astype(jnp.float32)).astype(jnp.bfloat16)
+            probs = jnp.sum(jnp.where(first == second, probs_ref[b], 0.0), axis=1, keepdims=True)
+            loads_og[b].wait()
+            source = (probs * held_og[b].astype(jnp.float32)).astype(jnp.bfloat16)
         chosen = jnp.dot(one_hot, source, preferred_element_type=jnp.float32)
         send[which, b] = chosen.astype(jnp.bfloat16).reshape(experts, capacity, width)
         recv[which, b, e] = send[which, b, e]
@@ -272,8 +295,9 @@
     fill(0, 0, one_hot)
     pl.semaphore_wait(barrier, experts + 1)
     each_peer(lambda k: dispatch(0, 0, k).start())
+    load_master.wait()
     for k in range(3):
-        weights[k, r] = master_ref[:, k * width : (k + 1) * width].astype(jnp.bfloat16)
+        weights[k, r] = held_master[:, k * width : (k + 1) * width].astype(jnp.bfloat16)
         weight_copy(1, k).start()
         weight_copy(0, k).start()
     fill(1, 0, one_hot)
@@ -294,46 +318,58 @@
     def matrix(k):
         return weights[k].reshape(total_units, width)
 
+    def weight_grad(k):
+        source = recv[k // 2].reshape(batches * rows, width)
+        total = jnp.dot(terms[k], source, preferred_element_type=jnp.float32)
+        total = total * (scale_hidden if k == 2 else scale_in)
+        part[k] = total.astype(jnp.bfloat16).reshape(4, units, width)
+        grad_copy(0, k).start()
+        grad_copy(1, k).start()
+
+    def over_x(k):
+        grad_copy(0, k).wait_recv()
+        chip_sum[k] = (
+            part[k, r_x].astype(jnp.float32) + sib[0, k].astype(jnp.float32)
+        ).astype(jnp.bfloat16)
+        grad_copy(2, k).start()
+
     for b in range(batches):
+        last = b == batches - 1
+        span = slice(b * rows, (b + 1) * rows)
         each_peer(lambda k: dispatch(0, b, k).wait_recv())
         x = recv[0, b].reshape(rows, width)
         gate = lax.dot_general(x, matrix(0), NT, preferred_element_type=jnp.float32) * scale_in
         up = lax.dot_general(x, matrix(1), NT, preferred_element_type=jnp.float32) * scale_in
         sig = jax.nn.sigmoid(gate)
         act = gate * sig
+        terms[2, :, span] = (act * up).T.astype(jnp.bfloat16)
         each_peer(lambda k: dispatch(1, b, k).wait_recv())
+        if last:
+            for done in range(b):
+                each_peer(lambda k: give_back(done, k).start())
+            weight_grad(2)
         g = recv[1, b].reshape(rows, width)
         hgrad = (
             lax.dot_general(g, matrix(2), NT, preferred_element_type=jnp.float32) * scale_hidden
         )
         up_grad = hgrad * act
         gate_grad = hgrad * up * sig * (1.0 + gate * (1.0 - sig))
-        gate_low, up_low = gate_grad.astype(jnp.bfloat16), up_grad.astype(jnp.bfloat16)
+        terms[0, :, span] = gate_grad.T.astype(jnp.bfloat16)
+        terms[1, :, span] = up_grad.T.astype(jnp.bfloat16)
+        if last:
+            over_x(2)
+            weight_grad(0)
+            weight_grad(1)
+            over_x(0)
         back = (
-            jnp.dot(gate_low, matrix(0), preferred_element_type=jnp.float32)
-            + jnp.dot(up_low, matrix(1), preferred_element_type=jnp.float32)
+            jnp.dot(gate_grad.astype(jnp.bfloat16), matrix(0), preferred_element_type=jnp.float32)
+            + jnp.dot(up_grad.astype(jnp.bfloat16), matrix(1), preferred_element_type=jnp.float32)
         ) * scale_in
         slots[b] = back.astype(jnp.bfloat16).reshape(experts, capacity, width)
-        each_peer(lambda k: give_back(b, k).start())
         ret[b, e] = slots[b, e]
-        span = slice(b * rows, (b + 1) * rows)
-        terms[0, :, span] = gate_grad.T.astype(jnp.bfloat16)
-        terms[1, :, span] = up_grad.T.astype(jnp.bfloat16)
-        terms[2, :, span] = (act * up).T.astype(jnp.bfloat16)
-
-    for k in range(3):
-        source = recv[k // 2].reshape(batches * rows, width)
-        total = jnp.dot(terms[k], source, preferred_element_type=jnp.float32)
-        total = total * (scale_hidden if k == 2 else scale_in)
-        part[k] = total.astype(jnp.bfloat16).reshape(4, units, width)
-        grad_copy(0, k).start()
-        grad_copy(1, k).start()
-    for k in range(3):
-        grad_copy(0, k).wait_recv()
-        chip_sum[k] = (
-            part[k, r_x].astype(jnp.float32) + sib[0, k].astype(jnp.float32)
-        ).astype(jnp.bfloat16)
-        grad_copy(2, k).start()
+        if last:
+            each_peer(lambda k: give_back(b, k).start())
+            over_x(1)
 
     for b in range(batches):
         each_peer(lambda k: give_back(b, k).wait_recv())
@@ -366,6 +402,7 @@
     peers = experts - 1
     low = jnp.bfloat16
     whole = pl.BlockSpec(memory_space=pltpu.VMEM)
+    far = pl.BlockSpec(memory_space=pltpu.HBM)
     dma = pltpu.SemaphoreType.DMA
     return pl.pallas_call(
         functools.partial(layer_kernel, experts, capacity),
@@ -373,9 +410,12 @@
             jax.ShapeDtypeStruct(inputs.shape, low),
             jax.ShapeDtypeStruct(master.shape, jnp.float32),
         ),
-        in_specs=[whole] * 5,
+        in_specs=[far, far, whole, whole, far],
         out_specs=(whole, whole),
         scratch_shapes=[
+            pltpu.VMEM(inputs.shape, low),
+            pltpu.VMEM(inputs.shape, low),
+            pltpu.VMEM(master.shape, jnp.float32),
             pltpu.VMEM((2, batches, experts, capacity, width), low),
             pltpu.VMEM((2, batches, experts, capacity, width), low),
             pltpu.VMEM((3, 4, units, width), low),
@@ -395,29 +435,98 @@
             dma((3, 3)),
             dma((3, 3)),
             dma((3, 3)),
+            dma((3, batches)),
         ],
         compiler_params=pltpu.CompilerParams(
-            collective_id=0, has_side_effects=True, vmem_limit_bytes=48 * 1024 * 1024
+            collective_id=0, has_side_effects=True, vmem_limit_bytes=61 * 1024 * 1024
         ),
         cost_estimate=pl.CostEstimate(
             flops=2 * 8 * batches * rows * 4 * units * width,
             bytes_accessed=8 * master.size,
             transcendentals=0,
         ),
-    )(inputs, out_grads, routes, gate_probs, master)
+    )(
+        inputs,
+        out_grads,
+        routes.reshape(batches, 1, tokens),
+        gate_probs.reshape(batches, 1, tokens),
+        master,
+    )
+
+
+def update_kernel(
+    ingrad_in, grad, master, moment, second, ingrad, nmaster, nmoment, nsecond, *scratch
+):
+    held, made, sems = scratch[:4], scratch[4:7], scratch[7]
+    depth = 16
+    pieces = grad.shape[0] // depth
+    spans = [pl.ds(i * depth, depth) for i in range(pieces)]
+    loads = [
+        [
+            pltpu.make_async_copy(source.at[span], place.at[span], sems.at[n, i])
+            for n, (source, place) in enumerate(zip((grad, master, moment, second), held))
+        ]
+        for i, span in enumerate(spans)
+    ]
+    for piece in loads:
+        for load in piece:
+            load.start()
+    rows_in = pltpu.make_async_copy(ingrad_in, scratch[8], sems.at[7, 0])
+    rows_in.start()
+    copies = []
+    for i, span in enumerate(spans):
+        for load in loads[i]:
+            load.wait()
+        values = adamw_step(held[1][span], held[2][span], held[3][span], held[0][span])
+        for n, target in enumerate((nmaster, nmoment, nsecond)):
+            made[n][span] = values[n]
+            copies.append(
+                pltpu.make_async_copy(made[n].at[span], target.at[span], sems.at[4 + n, i])
+            )
+            copies[-1].start()
+    rows_in.wait()
+    copies.append(pltpu.make_async_copy(scratch[8], ingrad, sems.at[7, 1]))
+    copies[-1].start()
+    for copy in copies:
+        copy.wait()
+
+
+def update(in_grads, grad_sum, master, moment, second):
+    far = pl.BlockSpec(memory_space=pltpu.HBM)
+    outs = [in_grads, master, moment, second]
+    return pl.pallas_call(
+        update_kernel,
+        out_shape=tuple(jax.ShapeDtypeStruct(o.shape, o.dtype) for o in outs),
+        in_specs=[far] * 5,
+        out_specs=(far,) * 4,
+        scratch_shapes=[
+            pltpu.VMEM(o.shape, o.dtype)
+            for o in (grad_sum, master, moment, second, master, moment, second)
+        ]
+        + [
+            pltpu.SemaphoreType.DMA((8, max(2, master.shape[0] // 16))),
+            pltpu.VMEM(in_grads.shape, in_grads.dtype),
+        ],
+        compiler_params=pltpu.CompilerParams(vmem_limit_bytes=61 * 1024 * 1024),
+        cost_estimate=pl.CostEstimate(
+            flops=16 * master.size, bytes_accessed=20 * master.size, transcendentals=master.size
+        ),
+    )(in_grads, grad_sum, master, moment, second)
 
 
 def on_device(inputs, out_grads, routes, gate_probs, master, moment, second):
     experts = lax.axis_size("expert")
     tokens = inputs.shape[1]
     capacity = max(2, 2 * tokens * routes.shape[2] // experts)
-    fits = capacity % 16 == 0 and experts * capacity % 128 == 0
+    fits = capacity % 16 == 0 and master.shape[1] % 16 == 0 and experts * capacity % 128 == 0
     if routes.shape[2] != 1 or lax.axis_size("replica") != 4 or not fits:
         return on_device_plain(inputs, out_grads, routes, gate_probs, master, moment, second)
     in_grads, grad_sum = fused_layer(
         experts, capacity, inputs, out_grads, routes, gate_probs, master[0]
     )
-    new_master, new_moment, new_second = adamw_step(master[0], moment[0], second[0], grad_sum)
+    in_grads, new_master, new_moment, new_second = update(
+        in_grads, grad_sum, master[0], moment[0], second[0]
+    )
     return (in_grads, new_master[None], new_moment[None], new_second[None])
 
 

time: 90.3 us -> 82.6 us (0.915)
  the two profiles are of different devices: /device:TPU:29 before, /device:TPU:0 now
where the time goes in v2:
time: 82.6 us; the launch traced here: 81.4 us
  Pallas kernels  80.7 us (98%)
    pallas_call x1, Pallas kernels, fused_layer(): pl.pallas_call(functools.partial(layer_kernel, experts, capacity), out_sh...  76.4 us
    pallas_call x1, Pallas kernels, update(): pl.pallas_call(update_kernel, out_shape=tuple((jax.ShapeDtypeStruct(o.sha...  4.36 us

profile of v2, /device:TPU:0, one launch (start us, length us, event | category | flops | bytes accessed | tf_op | source)
XLA Modules:
  0.0 81.4 jit_solution(14385664980352387284)
XLA Ops:
  0.6 76.4 %shard_map.102 = (bf16[2,64,2048]{2,1,0:T(8,128)(2,1)}, f32[64,6144]{1,0:T(8,128)}) custom-call(bf16[2,64,2048]{2,1,0:T(8,128)(2,1)} %in_ref.1, bf16[2,64,2048]{2,1,0:T(8,128)(2,1)} %og_ref.1, s32[2,1,64]{2,1,0:T(1,128)} %bitcast.19, f32[2,1,64]{2,1,0:T(1,128)} %bitcast.20, f32[64,6144]{1,0:T(8,128)} %bitcast.12), custom_call_target="tpu_custom_call" | custom-call | flops 2147483648 | bytes 3145728 | tf_op jit(solution)/shard_map/pallas_call | solution.py:407
  77.0 4.4 %shard_map.103 = (bf16[2,64,2048]{2,1,0:T(8,128)(2,1)}, f32[64,6144]{1,0:T(8,128)}, f32[64,6144]{1,0:T(8,128)}, bf16[64,6144]{1,0:T(8,128)(2,1)}) custom-call(bf16[2,64,2048]{2,1,0:T(8,128)(2,1)} %get-tuple-element.10.ingrad_in, f32[64,6144]{1,0:T(8,128)} %get-tuple-element.11.grad, f32[64,6144]{1,0:T(8,128)} %bitcast.13, f32[64,6144]{1,0:T(8,128)} %bitcast.14, ...), custom_call_target="tpu_custom_call" | custom-call | flops 6291456 | bytes 7864320 | tf_op jit(solution)/shard_map/pallas_call | solution.py:497

commit v3 on v2

--- a/solution.py
+++ b/solution.py
@@ -253,7 +253,7 @@
 
     def each_peer(step):
         def body(k, c):
-            step(k)
+            step(lax.rem(k, 2) * ((k + 1) // 2) + (1 - lax.rem(k, 2)) * (experts - k // 2))
             return c
 
         lax.fori_loop(1, experts, body, 0)

time: 82.6 us -> 84 us (1.017); the launches traced: 81.4 us -> 83.8 us
  Pallas kernels: 80.7 us -> 83.2 us
    pallas_call x1, Pallas kernels: 76.4 us -> 78.8 us  [fused_layer(): pl.pallas_call(functools.partial(layer_kernel, experts, capacity), out_sh...]
where the time goes in v3:
time: 84 us; the launch traced here: 83.8 us
  Pallas kernels  83.2 us (99%)
    pallas_call x1, Pallas kernels, fused_layer(): pl.pallas_call(functools.partial(layer_kernel, experts, capacity), out_sh...  78.8 us
    pallas_call x1, Pallas kernels, update(): pl.pallas_call(update_kernel, out_shape=tuple((jax.ShapeDtypeStruct(o.sha...  4.36 us

profile of v3, /device:TPU:0, one launch (start us, length us, event | category | flops | bytes accessed | tf_op | source)
XLA Modules:
  0.0 83.8 jit_solution(15623103055298847829)
XLA Ops:
  0.6 78.8 %shard_map.102 = (bf16[2,64,2048]{2,1,0:T(8,128)(2,1)}, f32[64,6144]{1,0:T(8,128)}) custom-call(bf16[2,64,2048]{2,1,0:T(8,128)(2,1)} %in_ref.1, bf16[2,64,2048]{2,1,0:T(8,128)(2,1)} %og_ref.1, s32[2,1,64]{2,1,0:T(1,128)} %bitcast.19, f32[2,1,64]{2,1,0:T(1,128)} %bitcast.20, f32[64,6144]{1,0:T(8,128)} %bitcast.12), custom_call_target="tpu_custom_call" | custom-call | flops 2147483648 | bytes 3145728 | tf_op jit(solution)/shard_map/pallas_call | solution.py:407
  79.5 4.4 %shard_map.103 = (bf16[2,64,2048]{2,1,0:T(8,128)(2,1)}, f32[64,6144]{1,0:T(8,128)}, f32[64,6144]{1,0:T(8,128)}, bf16[64,6144]{1,0:T(8,128)(2,1)}) custom-call(bf16[2,64,2048]{2,1,0:T(8,128)(2,1)} %get-tuple-element.10.ingrad_in, f32[64,6144]{1,0:T(8,128)} %get-tuple-element.11.grad, f32[64,6144]{1,0:T(8,128)} %bitcast.13, f32[64,6144]{1,0:T(8,128)} %bitcast.14, ...), custom_call_target="tpu_custom_call" | custom-call | flops 6291456 | bytes 7864320 | tf_op jit(solution)/shard_map/pallas_call | solution.py:497
